TPU v7x, 512 devices: a whole 4x4x16 slice. The times are simulated.
512 devices in a mesh: dp: 32 (over z, core), ctx: 16 (over y, x).
Axes of the slice: x: 4, y: 4, z: 16, core: 2. Of those that a mesh axis runs over, the one named last changes fastest.
Arguments:
- tokens: bfloat16 [4096, 7168], P('dp', 'ctx'), may hold values from -6 to 6
- routes: int32 [4096, 2], P('dp'), may hold values from 0 to 31, all different within a row; in each aligned block of 128 rows (0 to 127, 128 to 255, ...) at most 16 rows name the same one
- route_weights: float32 [4096, 2], P('dp'), may hold values from 0.2 to 1.5
- w_gate: bfloat16 [32, 7168, 1024], P('dp', 'ctx'), may hold values from -0.0625 to 0.0625
- w_up: bfloat16 [32, 7168, 1024], P('dp', 'ctx'), may hold values from -0.0625 to 0.0625
- w_down: bfloat16 [32, 1024, 7168], P('dp', None, 'ctx'), may hold values from -0.375 to 0.375
- cotangent: bfloat16 [4096, 7168], P('dp', 'ctx'), may hold values from -6 to 6
Outputs:
- mixed: bfloat16 [4096, 7168], P('dp', 'ctx')
- token_grad: bfloat16 [4096, 7168], P('dp', 'ctx')
Inputs may be any that keep to these rules, and one draw needn't show every extreme that they name: Within the tokens of one index of dp no expert is named by more than 16 routes, one expert exactly 16; the routes of a token name distinct experts.
All inputs are finite; a program needn't handle non-finite values.
Results may differ from a plain program's by a relative error of at most 0.03.
Values may be sent and summed in bfloat16 or wider, within the bound.
A program may use at most 64 MiB of HBM per device.

v0:
```python
import jax
import jax.numpy as jnp
from jax import lax
from jax.sharding import PartitionSpec as P


def slot_tables(routes, route_weights, experts, capacity):
    flat = routes.reshape(-1)
    onehot = (flat[:, None] == jnp.arange(experts, dtype=jnp.int32)[None, :]).astype(jnp.int32)
    before = jnp.cumsum(onehot, axis=0) - onehot
    slot = jnp.sum(before * onehot, axis=1)
    column = flat * capacity + slot
    hit = (column[None, :] == jnp.arange(experts * capacity, dtype=jnp.int32)[:, None]).astype(
        jnp.float32
    )
    pick = (
        hit.reshape(experts * capacity, routes.shape[0], routes.shape[1])
        .sum(-1)
        .astype(jnp.bfloat16)
    )
    slot_weight = jnp.sum(hit * route_weights.reshape(-1)[None, :], axis=1)
    return (pick, slot_weight, column)


def forward_rows(x_recv, wg, wu, wd, cols):
    rows = x_recv.reshape(-1, cols)
    gate_part = jnp.dot(rows, wg, preferred_element_type=jnp.float32)
    up_part = jnp.dot(rows, wu, preferred_element_type=jnp.float32)
    gate, up = (
        lax.psum(gate_part.astype(jnp.bfloat16), "ctx").astype(jnp.float32),
        lax.psum(up_part.astype(jnp.bfloat16), "ctx").astype(jnp.float32),
    )
    sig = jax.nn.sigmoid(gate)
    hidden = (gate * sig * up).astype(jnp.bfloat16)
    out_part = jnp.dot(hidden, wd, preferred_element_type=jnp.float32).astype(jnp.bfloat16)
    return (out_part.reshape(x_recv.shape), gate, up, sig)


def backward_rows(dy_recv, gate, up, sig, wg, wu, wd, cols):
    contract = (((1,), (1,)), ((), ()))
    grad_rows = dy_recv.reshape(-1, cols)
    grad_part = lax.dot_general(grad_rows, wd, contract, preferred_element_type=jnp.float32)
    hidden_grad = lax.psum(grad_part.astype(jnp.bfloat16), "ctx").astype(jnp.float32)
    gate_grad = (hidden_grad * up * sig * (1.0 + gate * (1.0 - sig))).astype(jnp.bfloat16)
    up_grad = (hidden_grad * gate * sig).astype(jnp.bfloat16)
    row_part = (
        lax.dot_general(gate_grad, wg, contract, preferred_element_type=jnp.float32)
        + lax.dot_general(up_grad, wu, contract, preferred_element_type=jnp.float32)
    ).astype(jnp.bfloat16)
    return row_part.reshape(dy_recv.shape)


def send_rows(values):
    return lax.all_to_all(values, "dp", split_axis=0, concat_axis=0, tiled=True)


def send_grads(values):
    return lax.all_to_all(values, "dp", split_axis=0, concat_axis=0, tiled=True)


def return_rows(values):
    return lax.all_to_all(values, "dp", split_axis=0, concat_axis=0, tiled=True)


def return_grads(values):
    return lax.all_to_all(values, "dp", split_axis=0, concat_axis=0, tiled=True)


def shards(tokens, routes, route_weights, w_gate, w_up, w_down, cotangent):
    experts = lax.axis_size("dp")
    tok_rows, top = routes.shape
    capacity = max(2, (2 * tok_rows * top + experts - 1) // experts)
    cols = tokens.shape[1]
    pick, slot_weight, column = slot_tables(routes, route_weights, experts, capacity)
    x_slots = jnp.dot(pick, tokens, preferred_element_type=jnp.float32).astype(jnp.bfloat16)
    dy_picked = jnp.dot(pick, cotangent, preferred_element_type=jnp.float32)
    dy_slots = (dy_picked * slot_weight[:, None]).astype(jnp.bfloat16)
    x_slots = x_slots.reshape(experts, capacity, cols)
    dy_slots = dy_slots.reshape(experts, capacity, cols)
    wg = w_gate[0]
    wu = w_up[0]
    wd = w_down[0]
    x_recv = send_rows(x_slots)
    out_part, gate, up, sig = forward_rows(x_recv, wg, wu, wd, cols)
    expert_out = return_rows(out_part)
    dy_recv = send_grads(dy_slots)
    row_part = backward_rows(dy_recv, gate, up, sig, wg, wu, wd, cols)
    row_grad = return_grads(row_part)
    expert_flat = expert_out.reshape(experts * capacity, cols)
    grad_flat = row_grad.reshape(experts * capacity, cols)
    out_routes = expert_flat[column].astype(jnp.float32).reshape(tok_rows, top, cols)
    grad_routes = grad_flat[column].astype(jnp.float32).reshape(tok_rows, top, cols)
    mixed = jnp.sum(out_routes * route_weights[:, :, None], axis=1).astype(jnp.bfloat16)
    token_grad = jnp.sum(grad_routes, axis=1).astype(jnp.bfloat16)
    return (mixed, token_grad)


def solution(mesh):
    in_specs = (
        P("dp", "ctx"),
        P("dp", None),
        P("dp", None),
        P("dp", "ctx", None),
        P("dp", "ctx", None),
        P("dp", None, "ctx"),
        P("dp", "ctx"),
    )
    out_specs = (P("dp", "ctx"), P("dp", "ctx"))
    return jax.shard_map(shards, mesh=mesh, in_specs=in_specs, out_specs=out_specs, check_vma=False)
```

profile of v0, /device:TPU:1, one launch (start us, length us, event | category | flops | bytes accessed | tf_op | source)
XLA Modules:
  0.0 320.1 jit_solution(4032728329189671781)
XLA Ops:
  7.2 0.0 copy-start
  7.2 0.9 copy.35
  8.0 0.1 eq.45
  8.2 0.1 eq.49
  8.3 0.6 reduce-window.6
  8.9 0.2 slice_reduce_fusion
  9.2 0.1 fusion.26
  9.3 0.1 reduce_sum.53
  9.4 0.1 copy.39
  9.5 0.1 convert_reduce_fusion
  9.6 1.2 convolution_convert_fusion.4
  10.8 0.0 copy-start.2
  10.8 0.0 copy-start.1
  10.8 1.0 copy.40
  11.8 16.7 %all-to-all-start = ((bf16[32,16,448]{2,1,0:T(8,128)(2,1)}), bf16[32,16,448]{2,1,0:T(8,128)(2,1)S(1)}, u32[]{:S(2)}, u32[]{:S(2)}) async-start(bf16[32,16,448]{2,1,0:T(8,128)(2,1)} %bitcast.1), calls=%async_computation | async-start | bytes 1048576 | tf_op jit(solution)/shard_map/all_to_all | solution.py:54
  28.6 0.1 copy.42
  28.7 0.1 mul.88
  28.9 0.1 select_reduce_fusion
  29.0 0.3 fusion.10
  29.3 0.0 copy-start.6
  29.3 1.0 copy.44
  30.3 31.8 %all-to-all-done = bf16[32,16,448]{2,1,0:T(8,128)(2,1)S(1)} async-done(((bf16[32,16,448]{2,1,0:T(8,128)(2,1)}), bf16[32,16,448]{2,1,0:T(8,128)(2,1)S(1)}, u32[]{:S(2)}, u32[]{:S(2)}) %all-to-all-start) | async-done | bytes 458784 | tf_op jit(solution)/shard_map/all_to_all | solution.py:54
  62.1 4.0 %all-to-all-start.2 = ((bf16[32,16,448]{2,1,0:T(8,128)(2,1)}), bf16[32,16,448]{2,1,0:T(8,128)(2,1)S(1)}, u32[]{:S(2)}, u32[]{:S(2)}) async-start(bf16[32,16,448]{2,1,0:T(8,128)(2,1)} %bitcast.10), calls=%async_computation.2 | async-start | bytes 1048576 | tf_op jit(solution)/shard_map/all_to_all | solution.py:58
  66.1 0.0 all-reduce.3.cloned.1.call-start
  66.2 1.7 convolution_convert_fusion.1
  67.9 1.7 convolution_convert_fusion.2
  69.6 30.1 %all-to-all-done.2 = bf16[32,16,448]{2,1,0:T(8,128)(2,1)S(1)} async-done(((bf16[32,16,448]{2,1,0:T(8,128)(2,1)}), bf16[32,16,448]{2,1,0:T(8,128)(2,1)S(1)}, u32[]{:S(2)}, u32[]{:S(2)}) %all-to-all-start.2) | async-done | bytes 458784 | tf_op jit(solution)/shard_map/all_to_all | solution.py:58
  99.7 2.9 convolution_convert_fusion
  102.6 0.0 all-reduce.3.cloned.1.call-update
  102.6 117.9 %all-reduce.3.cloned.1.call-done = (bf16[512,1024]{1,0:T(8,128)(2,1)}, bf16[512,1024]{1,0:T(8,128)(2,1)}, bf16[512,1024]{1,0:T(8,128)(2,1)}) async-done(((bf16[512,1024]{1,0:T(8,128)(2,1)}, bf16[512,1024]{1,0:T(8,128)(2,1)}, bf16[512,1024]{1,0:T(8,128)(2,1)}), (bf16[512,1024]{1,0:T(8,128)(2,1)}, bf16[512,1024]{1,0:T(8,128)(2,1)}, bf16[512,1024]{1,0:T(8,128)(2,1)})) %all-reduce.3.cloned.1.call-update) | async-done | bytes 3145744 | tf_op jit(solution)/shard_map/psum | solution.py:31
  220.5 3.3 %fusion.14 = f32[512,448]{0,1:T(8,128)S(1)} fusion(bf16[512,1024]{1,0:T(8,128)(2,1)} %get-tuple-element.6, bf16[512,1024]{1,0:T(8,128)(2,1)} %get-tuple-element.8, bf16[512,1024]{1,0:T(8,128)(2,1)} %get-tuple-element.7, bf16[1,448,1024]{2,1,0:T(8,128)(2,1)S(1)} %copy-done), kind=kOutput, calls=%fused_computation.27 | convolution fusion | flops 476577792 | bytes 4980736 | tf_op jit(solution)/shard_map/dot_general | solution.py:47
  223.8 1.0 fusion.11
  224.8 1.0 copy.45
  225.8 13.3 %all-to-all-start.3 = ((bf16[32,16,448]{2,1,0:T(8,128)(2,1)}), bf16[32,16,448]{2,1,0:T(8,128)(2,1)S(1)}, u32[]{:S(2)}, u32[]{:S(2)}) async-start(bf16[32,16,448]{2,1,0:T(8,128)(2,1)} %bitcast.12), calls=%async_computation.3 | async-start | bytes 1048576 | tf_op jit(solution)/shard_map/all_to_all | solution.py:66
  239.2 2.5 convolution_convert_fusion.3
  241.6 1.0 copy.41
  242.6 30.0 %all-to-all-done.3 = bf16[32,16,448]{2,1,0:T(8,128)(2,1)S(1)} async-done(((bf16[32,16,448]{2,1,0:T(8,128)(2,1)}), bf16[32,16,448]{2,1,0:T(8,128)(2,1)S(1)}, u32[]{:S(2)}, u32[]{:S(2)}) %all-to-all-start.3) | async-done | bytes 458784 | tf_op jit(solution)/shard_map/all_to_all | solution.py:66
  272.7 4.0 %all-to-all-start.1 = ((bf16[32,16,448]{2,1,0:T(8,128)(2,1)}), bf16[32,16,448]{2,1,0:T(8,128)(2,1)S(1)}, u32[]{:S(2)}, u32[]{:S(2)}) async-start(bf16[32,16,448]{2,1,0:T(8,128)(2,1)} %bitcast.6), calls=%async_computation.1 | async-start | bytes 1048576 | tf_op jit(solution)/shard_map/all_to_all | solution.py:62
  276.7 0.1 mul.83
  276.9 1.2 gather_fusion.1
  278.0 0.1 gather.10
  278.1 0.7 reduce_sum.58
  278.9 0.8 copy.47
  279.6 30.6 %all-to-all-done.1 = bf16[32,16,448]{2,1,0:T(8,128)(2,1)S(1)} async-done(((bf16[32,16,448]{2,1,0:T(8,128)(2,1)}), bf16[32,16,448]{2,1,0:T(8,128)(2,1)S(1)}, u32[]{:S(2)}, u32[]{:S(2)}) %all-to-all-start.1) | async-done | bytes 458784 | tf_op jit(solution)/shard_map/all_to_all | solution.py:62
  310.2 1.2 gather_fusion
  311.4 0.3 reshape.110
  311.7 0.7 multiply_reduce_fusion
  312.5 0.8 copy.46
  (17 shorter events, 0.1 us)
Async XLA Ops:
  7.2 60.7 %copy-start = (bf16[1,448,1024]{2,1,0:T(8,128)(2,1)S(1)}, bf16[1,448,1024]{2,1,0:T(8,128)(2,1)}, u32[]{:S(2)}) copy-start(bf16[1,448,1024]{2,1,0:T(8,128)(2,1)} %param.10) | copy-start | bytes 2752516
  10.8 17.8 %copy-start.2 = (f32[128,2]{0,1:T(2,128)S(1)}, f32[128,2]{0,1:T(2,128)}, u32[]{:S(2)}) copy-start(f32[128,2]{0,1:T(2,128)} %param.9) | copy-start | bytes 3076
  10.8 18.2 %copy-start.1 = (bf16[128,448]{0,1:T(8,128)(2,1)S(1)}, bf16[128,448]{0,1:T(8,128)(2,1)}, u32[]{:S(2)}) copy-start(bf16[128,448]{0,1:T(8,128)(2,1)} %param.13) | copy-start | bytes 344068
  11.8 50.3 %all-to-all-start = ((bf16[32,16,448]{2,1,0:T(8,128)(2,1)}), bf16[32,16,448]{2,1,0:T(8,128)(2,1)S(1)}, u32[]{:S(2)}, u32[]{:S(2)}) async-start(bf16[32,16,448]{2,1,0:T(8,128)(2,1)} %bitcast.1), calls=%async_computation | async-start | bytes 1048576 | tf_op jit(solution)/shard_map/all_to_all | solution.py:54
  29.3 36.9 %copy-start.6 = (bf16[1,448,1024]{2,1,0:T(8,128)(2,1)S(1)}, bf16[1,448,1024]{2,1,0:T(8,128)(2,1)}, u32[]{:S(2)}) copy-start(bf16[1,448,1024]{2,1,0:T(8,128)(2,1)} %param.11) | copy-start | bytes 2752516
  62.1 37.6 %all-to-all-start.2 = ((bf16[32,16,448]{2,1,0:T(8,128)(2,1)}), bf16[32,16,448]{2,1,0:T(8,128)(2,1)S(1)}, u32[]{:S(2)}, u32[]{:S(2)}) async-start(bf16[32,16,448]{2,1,0:T(8,128)(2,1)} %bitcast.10), calls=%async_computation.2 | async-start | bytes 1048576 | tf_op jit(solution)/shard_map/all_to_all | solution.py:58
  66.1 154.4 %all-reduce.3.cloned.1.call-start = ((), (), s32[]{:S(2)}) async-start(), calls=%async_computation.4 | async-start | bytes 6291456 | tf_op jit(solution)/shard_map/psum | solution.py:31
  220.5 3.3 %copy-start.4 = (bf16[512,1024]{1,0:T(8,128)(2,1)S(1)}, bf16[512,1024]{1,0:T(8,128)(2,1)}, u32[]{:S(2)}) copy-start(bf16[512,1024]{1,0:T(8,128)(2,1)} %get-tuple-element.7) | copy-start | bytes 3145732
  220.5 3.3 %copy-start.5 = (bf16[512,1024]{1,0:T(8,128)(2,1)S(1)}, bf16[512,1024]{1,0:T(8,128)(2,1)}, u32[]{:S(2)}) copy-start(bf16[512,1024]{1,0:T(8,128)(2,1)} %get-tuple-element.8) | copy-start | bytes 3145732
  224.8 14.3 %copy-start.3 = (bf16[512,1024]{1,0:T(8,128)(2,1)S(1)}, bf16[512,1024]{1,0:T(8,128)(2,1)}, u32[]{:S(2)}) copy-start(bf16[512,1024]{1,0:T(8,128)(2,1)} %get-tuple-element.6) | copy-start | bytes 3145732
  225.8 46.8 %all-to-all-start.3 = ((bf16[32,16,448]{2,1,0:T(8,128)(2,1)}), bf16[32,16,448]{2,1,0:T(8,128)(2,1)S(1)}, u32[]{:S(2)}, u32[]{:S(2)}) async-start(bf16[32,16,448]{2,1,0:T(8,128)(2,1)} %bitcast.12), calls=%async_computation.3 | async-start | bytes 1048576 | tf_op jit(solution)/shard_map/all_to_all | solution.py:66
  272.7 37.6 %all-to-all-start.1 = ((bf16[32,16,448]{2,1,0:T(8,128)(2,1)}), bf16[32,16,448]{2,1,0:T(8,128)(2,1)S(1)}, u32[]{:S(2)}, u32[]{:S(2)}) async-start(bf16[32,16,448]{2,1,0:T(8,128)(2,1)} %bitcast.6), calls=%async_computation.1 | async-start | bytes 1048576 | tf_op jit(solution)/shard_map/all_to_all | solution.py:62
Sparse Core Ops, SparseCore 0:
  102.7 117.7 all-reduce.2
where the time goes:
time: 321 us; the launch traced here: 320 us
  waiting for transfers between devices  240 us (75%)
  starting transfers between devices  38.2 us (12%)
  matrix products  14.5 us (5%)
  between operations  14.3 us (4%)
  local copies, waits for them, and re-layouts  10.3 us (3%)
    psum x1, waiting for transfers between devices, forward_rows(): lax.psum(up_part.astype(jnp.bfloat16), 'ctx').astype(jnp.float32)  118 us
    all_to_all x1, waiting for transfers between devices, send_rows(): return lax.all_to_all(values, 'dp', split_axis=0, concat_axis=0, tiled=True)  31.8 us
    all_to_all x1, waiting for transfers between devices, return_rows(): return lax.all_to_all(values, 'dp', split_axis=0, concat_axis=0, tiled=True)  30.6 us
    all_to_all x1, waiting for transfers between devices, send_grads(): return lax.all_to_all(values, 'dp', split_axis=0, concat_axis=0, tiled=True)  30.1 us
    all_to_all x1, waiting for transfers between devices, return_grads(): return lax.all_to_all(values, 'dp', split_axis=0, concat_axis=0, tiled=True)  30 us
    all_to_all x1, starting transfers between devices, send_rows(): return lax.all_to_all(values, 'dp', split_axis=0, concat_axis=0, tiled=True)  16.7 us
    all_to_all x1, starting transfers between devices, return_grads(): return lax.all_to_all(values, 'dp', split_axis=0, concat_axis=0, tiled=True)  13.3 us
  transfers between devices with their start and end apart: 5, of which 5 were waited for; matrix products, arithmetic and copies ran while one was open for 4% of the time, Pallas kernels for 0%

commit v1 on v0

v1 whole, which is shorter than its diff:
```python
import functools

import jax
import jax.numpy as jnp
from jax import lax
from jax.experimental import pallas as pl
from jax.experimental.pallas import tpu as pltpu
from jax.sharding import PartitionSpec as P

MESH = pl.DeviceIdType.MESH
BF = jnp.bfloat16
F32 = jnp.float32

NZ = 16
NDP = 32
CAP = 16
NB = 8
COLS = 448
PAIR = 2 * COLS
FF = 1024
PAD = 64


def chip_at(z, k):
    off = ((k + 1) // 2) * (2 * (k % 2) - 1)
    return (z + NZ + off) % NZ


def mirror(k):
    odd = k % 2
    inner = jnp.where((k == 0) | (k == NZ - 1), 0, 2 * odd - 1)
    return k + inner


def nt(a, b):
    return lax.dot_general(a, b, (((1,), (1,)), ((), ())), preferred_element_type=F32)


def nn(a, b):
    return jnp.dot(a, b, preferred_element_type=F32)


def kernel(
    tok_hbm, routes_ref, rw_ref, wg_hbm, wu_hbm, wd_hbm, cot_hbm,
    mixed_ref, grad_ref,
    tok, cot, wd_in, wg, wu, wd_l, wd_r,
    xs, xr, p1s, p1r, p2s, p2r, h1, h2, rs, rr, pt0, pt1,
    in_sem, send_sem, x_sem, p1_sem, p2_sem, h1_sem, h2_sem, r_sem,
):
    dp = lax.axis_index("dp")
    ctx = lax.axis_index("ctx")
    z, y, x = dp // 2, ctx // 4, ctx % 4

    barrier = pltpu.get_barrier_semaphore()

    def greet_dp(k, carry):
        pl.semaphore_signal(barrier, inc=1, device_id={"dp": (dp + k) % NDP}, device_id_type=MESH)
        return carry

    def greet_ctx(k, carry):
        pl.semaphore_signal(barrier, inc=1, device_id={"ctx": (ctx + k) % 16}, device_id_type=MESH)
        return carry

    loads = [
        pltpu.make_async_copy(tok_hbm, tok, in_sem.at[0]),
        pltpu.make_async_copy(cot_hbm, cot, in_sem.at[1]),
        pltpu.make_async_copy(wg_hbm, wg.at[pl.ds(PAD, COLS)], in_sem.at[2]),
        pltpu.make_async_copy(wu_hbm, wu.at[pl.ds(PAD, COLS)], in_sem.at[3]),
        pltpu.make_async_copy(wd_hbm, wd_in, in_sem.at[4]),
    ]
    lax.fori_loop(1, NDP, greet_dp, 0)
    lax.fori_loop(1, 16, greet_ctx, 0)
    for load in loads:
        load.start()

    r0, r1 = routes_ref[:, 0:1], routes_ref[:, 1:2]
    w0, w1 = rw_ref[:, 0:1], rw_ref[:, 1:2]
    rows = routes_ref.shape[0]
    experts = lax.broadcasted_iota(jnp.int32, (rows, 128), 1)
    oh0 = (r0 == experts).astype(F32)
    oh1 = (r1 == experts).astype(F32)
    earlier = (
        lax.broadcasted_iota(jnp.int32, (rows, rows), 1)
        < lax.broadcasted_iota(jnp.int32, (rows, rows), 0)
    ).astype(F32)
    before = nn(earlier.astype(BF), (oh0 + oh1).astype(BF))
    s0 = jnp.sum(before * oh0, axis=1, keepdims=True).astype(jnp.int32)
    s1 = jnp.sum(before * oh1, axis=1, keepdims=True).astype(jnp.int32)
    places = lax.broadcasted_iota(jnp.int32, (rows, NDP * CAP), 1)
    hit0 = (r0 * CAP + s0 == places).astype(F32)
    hit1 = (r1 * CAP + s1 == places).astype(F32)
    pt0[...] = hit0
    pt1[...] = hit1
    loads[0].wait()
    loads[1].wait()
    cot_f = cot[...].astype(F32)
    both = jnp.concatenate(
        [
            jnp.concatenate([tok[...].astype(F32), cot_f * w0], axis=1),
            jnp.concatenate([tok[...].astype(F32), cot_f * w1], axis=1),
        ],
        axis=0,
    ).astype(BF)
    pick = jnp.concatenate([hit0, hit1], axis=0).T.astype(BF)
    xs[...] = nn(pick, both).astype(BF).reshape(NDP, CAP, PAIR)

    pl.semaphore_wait(barrier, NDP - 1 + 15)

    def dispatch(k, carry):
        chip = chip_at(z, k)
        place = mirror(k)
        for core in range(2):
            dst = chip * 2 + core

            @pl.when(dst != dp)
            def _():
                pltpu.make_async_remote_copy(
                    src_ref=xs.at[dst], dst_ref=xr.at[dp], send_sem=send_sem.at[0],
                    recv_sem=x_sem.at[place], device_id={"dp": dst}, device_id_type=MESH,
                ).start()

        return carry

    lax.fori_loop(0, NZ, dispatch, 0)
    xr[dp] = xs[dp]

    zero = jnp.zeros((PAD, FF), BF)
    for w in (wg, wu):
        w[0:PAD] = zero
        w[PAD + COLS :] = zero
    loads[4].wait()

    def widen(i, carry):
        part = pl.ds(pl.multiple_of(i * 128, 128), 128)
        block = wd_in[part].astype(F32)
        blank = jnp.zeros((128, PAD), F32)
        wd_l[part] = jnp.concatenate([blank, block], axis=1).astype(BF)
        wd_r[part] = jnp.concatenate([block, blank], axis=1).astype(BF)
        return carry

    lax.fori_loop(0, FF // 128, widen, 0)
    loads[2].wait()
    loads[3].wait()

    def peer(along_x, d):
        if along_x:
            return y * 4 + (x + d) % 4
        return ((y + d) % 4) * 4 + x

    def send(src, dst, kind, recv, along_x, d):
        pltpu.make_async_remote_copy(
            src_ref=src, dst_ref=dst, send_sem=send_sem.at[kind], recv_sem=recv,
            device_id={"ctx": peer(along_x, d)}, device_id_type=MESH,
        ).start()

    def await_bytes(ref, sem):
        pltpu.make_async_copy(ref, ref, sem).wait()

    def first(g):
        return x if g == 0 else y

    def second(g):
        return y if g == 0 else x

    def products(b):
        @pl.when(b == 0)
        def _():
            await_bytes(xr.at[pl.ds(0, 1)], x_sem.at[0])

        @pl.when(b > 0)
        def _():
            await_bytes(xr.at[pl.ds(0, 2)], x_sem.at[2 * b])

        await_bytes(xr.at[pl.ds(0, 2)], x_sem.at[2 * b + 1])
        block = jnp.concatenate(
            [
                xr[pl.ds(2 * chip_at(z, 2 * b + g), 2)].reshape(2 * CAP, PAIR)
                for g in range(2)
            ],
            axis=0,
        )
        left, right = block[:, 0:512], block[:, 384:896]
        parts = (
            nn(left, wg[PAD : PAD + 512]),
            nn(left, wu[PAD : PAD + 512]),
            nt(right, wd_l[...]),
        )
        for g in range(2):
            for p in range(4):
                for a in range(3):
                    p1s[b, g, p, :, a * 256 : a * 256 + 256] = parts[a][
                        g * 32 : g * 32 + 32, p * 256 : p * 256 + 256
                    ].astype(BF)
        for d in range(1, 4):
            for g in range(2):
                send(
                    p1s.at[b, g, (first(g) + d) % 4], p1r.at[b, g, d - 1], 1, p1_sem.at[b], g == 0, d
                )

    def add_first(b):
        await_bytes(p1r.at[b], p1_sem.at[b])
        for g in range(2):
            total = p1s[b, g, first(g)].astype(F32)
            for d in range(3):
                total = total + p1r[b, g, d].astype(F32)
            for q in range(4):
                for a in range(3):
                    lane = a * 256 + 128 * (q % 2)
                    p2s[b, g, q, :, a * 128 : a * 128 + 128] = total[
                        16 * (q // 2) : 16 * (q // 2) + 16, lane : lane + 128
                    ].astype(BF)
        for d in range(1, 4):
            for g in range(2):
                send(
                    p2s.at[b, g, (second(g) + d) % 4], p2r.at[b, g, d - 1], 2, p2_sem.at[b], g == 1, d
                )

    def add_second(b):
        await_bytes(p2r.at[b], p2_sem.at[b])
        for g in range(2):
            total = p2s[b, g, second(g)].astype(F32)
            for d in range(3):
                total = total + p2r[b, g, d].astype(F32)
            gate, up, hidden_grad = total[:, 0:128], total[:, 128:256], total[:, 256:384]
            sig = jax.nn.sigmoid(gate)
            h1[b, g, second(g), :, 0:128] = (gate * sig * up).astype(BF)
            h1[b, g, second(g), :, 128:256] = (
                hidden_grad * up * sig * (1.0 + gate * (1.0 - sig))
            ).astype(BF)
            h1[b, g, second(g), :, 256:384] = (hidden_grad * gate * sig).astype(BF)
        for d in range(1, 4):
            for g in range(2):
                mine = h1.at[b, g, second(g)]
                send(mine, mine, 3, h1_sem.at[b], g == 1, d)

    def spread(b):
        await_bytes(p2r.at[b], h1_sem.at[b])
        for d in range(1, 4):
            for g in range(2):
                send(h1.at[b, g], h2.at[b, g, first(g)], 4, h2_sem.at[b], g == 0, d)
        for g in range(2):
            h2[b, g, first(g)] = h1[b, g]

    def give_back(b):
        await_bytes(p1r.at[b], h2_sem.at[b])

        def whole(a):
            return jnp.concatenate(
                [
                    jnp.concatenate(
                        [
                            h2[b, g, p, 2 * half + q, :, a * 128 : a * 128 + 128]
                            for p in range(4)
                            for q in range(2)
                        ],
                        axis=1,
                    )
                    for g in range(2)
                    for half in range(2)
                ],
                axis=0,
            )

        out = nn(whole(0), wd_r[...])
        row_grad = nt(whole(1), wg[0:512]) + nt(whole(2), wu[0:512])
        pair = jnp.concatenate(
            [out[:, 0:384], out[:, 384:512] + row_grad[:, 0:128], row_grad[:, 128:512]], axis=1
        ).astype(BF)
        for g in range(2):
            for core in range(2):
                dst = chip_at(z, 2 * b + g) * 2 + core
                at = (2 * g + core) * CAP
                rs[dst] = pair[at : at + CAP]

                @pl.when(dst != dp)
                def _():
                    pltpu.make_async_remote_copy(
                        src_ref=rs.at[dst], dst_ref=rr.at[dp], send_sem=send_sem.at[5],
                        recv_sem=r_sem.at[0], device_id={"dp": dst}, device_id_type=MESH,
                    ).start()

    stages = (products, add_first, add_second, spread, give_back)

    def step(t, carry):
        for s in reversed(range(len(stages))):
            b = t - s

            @pl.when((b >= 0) & (b < NB))
            def _():
                stages[s](b)

        return carry

    lax.fori_loop(0, NB + len(stages) - 1, step, 0)
    rr[dp] = rs[dp]

    hit0, hit1 = pt0[...], pt1[...]
    weighted = hit0 * rw_ref[:, 0:1] + hit1 * rw_ref[:, 1:2]
    high = weighted.astype(BF)
    low = (weighted - high.astype(F32)).astype(BF)
    plain = (hit0 + hit1).astype(BF)
    await_bytes(rr.at[pl.ds(0, NDP - 1)], r_sem.at[0])
    back = rr[...].reshape(NDP * CAP, PAIR)
    mixed_ref[...] = (nn(high, back[:, 0:512]) + nn(low, back[:, 0:512]))[:, 0:COLS].astype(BF)
    grad_ref[...] = nn(plain, back[:, 384:896])[:, PAD:].astype(BF)

    await_bytes(xs.at[pl.ds(0, NDP - 1)], send_sem.at[0])
    await_bytes(p1r, send_sem.at[1])
    await_bytes(p2r, send_sem.at[2])
    await_bytes(p2r, send_sem.at[3])
    await_bytes(p1r, send_sem.at[4])
    await_bytes(xs.at[pl.ds(0, NDP - 1)], send_sem.at[5])


def shards(tokens, routes, route_weights, w_gate, w_up, w_down, cotangent):
    rows, cols = tokens.shape
    hbm = pl.BlockSpec(memory_space=pl.ANY)
    vmem = pl.BlockSpec(memory_space=pltpu.VMEM)
    dma = pltpu.SemaphoreType.DMA
    out = jax.ShapeDtypeStruct((rows, cols), BF)
    return pl.pallas_call(
        kernel,
        out_shape=(out, out),
        in_specs=[hbm, vmem, vmem, hbm, hbm, hbm, hbm],
        out_specs=(vmem, vmem),
        scratch_shapes=[
            pltpu.VMEM((rows, cols), BF),
            pltpu.VMEM((rows, cols), BF),
            pltpu.VMEM((FF, COLS), BF),
            pltpu.VMEM((PAD + COLS + PAD, FF), BF),
            pltpu.VMEM((PAD + COLS + PAD, FF), BF),
            pltpu.VMEM((FF, 512), BF),
            pltpu.VMEM((FF, 512), BF),
            pltpu.VMEM((NDP, CAP, PAIR), BF),
            pltpu.VMEM((NDP, CAP, PAIR), BF),
            pltpu.VMEM((NB, 2, 4, 32, 768), BF),
            pltpu.VMEM((NB, 2, 3, 32, 768), BF),
            pltpu.VMEM((NB, 2, 4, 16, 384), BF),
            pltpu.VMEM((NB, 2, 3, 16, 384), BF),
            pltpu.VMEM((NB, 2, 4, 16, 384), BF),
            pltpu.VMEM((NB, 2, 4, 4, 16, 384), BF),
            pltpu.VMEM((NDP, CAP, PAIR), BF),
            pltpu.VMEM((NDP, CAP, PAIR), BF),
            pltpu.VMEM((rows, NDP * CAP), F32),
            pltpu.VMEM((rows, NDP * CAP), F32),
            dma((5,)),
            dma((6,)),
            dma((NZ,)),
            dma((NB,)),
            dma((NB,)),
            dma((NB,)),
            dma((NB,)),
            dma((1,)),
        ],
        compiler_params=pltpu.CompilerParams(
            collective_id=0, has_side_effects=True, vmem_limit_bytes=48 << 20
        ),
        cost_estimate=pl.CostEstimate(
            flops=6 * 2 * 512 * COLS * FF, bytes_accessed=4 << 20, transcendentals=1 << 16
        ),
    )(tokens, routes, route_weights, w_gate[0], w_up[0], w_down[0], cotangent)


def solution(mesh):
    in_specs = (
        P("dp", "ctx"),
        P("dp", None),
        P("dp", None),
        P("dp", "ctx", None),
        P("dp", "ctx", None),
        P("dp", None, "ctx"),
        P("dp", "ctx"),
    )
    out_specs = (P("dp", "ctx"), P("dp", "ctx"))
    return jax.shard_map(shards, mesh=mesh, in_specs=in_specs, out_specs=out_specs, check_vma=False)
```

time: 321 us -> 112 us (0.35)
  the two profiles are of different devices: /device:TPU:1 before, /device:TPU:97 now
where the time goes in v1:
time: 112 us
  Pallas kernels  105 us (94%)
  local copies, waits for them, and re-layouts  5.84 us (5%)
    pallas_call x1, Pallas kernels, shards(): pl.pallas_call(kernel, out_shape=(out, out), in_specs=[hbm, vmem, vmem, h...  105 us
    unnamed x13, local copies, waits for them, and re-layouts  4.31 us

profile of v1, /device:TPU:97, one launch (start us, length us, event | category | flops | bytes accessed | tf_op | source)
XLA Modules:
  0.0 112.0 jit_solution(5017790313234086559)
XLA Ops:
  0.6 0.0 copy-start.2
  0.6 0.8 copy.11.routes_ref
  1.5 0.8 copy.12.rw_ref
  2.2 0.0 copy-done.2
  2.2 0.0 copy-start.3
  2.3 0.1 copy.10.tok_hbm
  2.4 0.8 copy-done.3
  3.2 0.1 copy.13.cot_hbm
  3.3 0.0 copy-start
  3.3 0.0 copy-start.1
  3.3 1.6 %copy.9 = bf16[1,1024,448]{2,1,0:T(8,128)(2,1)S(1)} copy(bf16[1,1024,448]{1,2,0:T(8,128)(2,1)} %param.12) | data formatting | bytes 1835008 | tf_op args[5]
  4.9 0.0 copy-done
  4.9 0.1 copy-done.1
  5.0 105.5 %shard_map.86 = (bf16[128,448]{1,0:T(8,128)(2,1)S(1)}, bf16[128,448]{1,0:T(8,128)(2,1)S(1)}) custom-call(bf16[128,448]{1,0:T(8,128)(2,1)S(1)} %copy.10.tok_hbm, s32[128,2]{1,0:T(8,128)S(1)} %copy.11.routes_ref, f32[128,2]{1,0:T(8,128)S(1)} %copy.12.rw_ref, bf16[448,1024]{1,0:T(8,128)(2,1)S(1)} %bitcast.4, bf16[448,1024]{1,0:T(8,128)(2,1)S(1)} %bitcast.5, ...), custom_call_target="tpu_custom_call" | custom-call | flops 2818572288 | bytes 4194304 | tf_op jit(solution)/shard_map/pallas_call | solution.py:321
  110.5 0.8 copy.14
  111.3 0.8 copy.15
Async XLA Ops:
  0.6 1.6 %copy-start.2 = (bf16[128,448]{0,1:T(8,128)(2,1)S(1)}, bf16[128,448]{0,1:T(8,128)(2,1)}, u32[]{:S(2)}) copy-start(bf16[128,448]{0,1:T(8,128)(2,1)} %param.7) | copy-start | bytes 344068
  2.2 0.9 copy-start.3
  3.3 1.6 %copy-start = (bf16[1,448,1024]{2,1,0:T(8,128)(2,1)S(1)}, bf16[1,448,1024]{2,1,0:T(8,128)(2,1)}, u32[]{:S(2)}) copy-start(bf16[1,448,1024]{2,1,0:T(8,128)(2,1)} %param.10) | copy-start | bytes 2752516
  3.3 1.7 %copy-start.1 = (bf16[1,448,1024]{2,1,0:T(8,128)(2,1)S(1)}, bf16[1,448,1024]{2,1,0:T(8,128)(2,1)}, u32[]{:S(2)}) copy-start(bf16[1,448,1024]{2,1,0:T(8,128)(2,1)} %param.11) | copy-start | bytes 2752516

commit v2 on v1

v2 whole, which is shorter than its diff:
```python
import functools

import jax
import jax.numpy as jnp
from jax import lax
from jax.experimental import pallas as pl
from jax.experimental.pallas import tpu as pltpu
from jax.sharding import PartitionSpec as P

LOGICAL = pl.DeviceIdType.LOGICAL
BF = jnp.bfloat16
F32 = jnp.float32

NZ = 16
NDP = 32
CAP = 16
NB = 8
COLS = 448
PAIR = 2 * COLS
FF = 1024
PAD = 64


FAR = (2, 7, 6, 5, 4, 3, 1, 0)
PLAN = (
    (0, 0), (1, 0), (2, 0), (0, 1), (3, 0), (1, 1), (0, 2), (4, 0),
    (2, 1), (1, 2), (3, 1), (0, 3), (2, 2), (4, 1), (1, 3), (3, 2),
    (0, 4), (2, 3), (4, 2), (0, 5), (3, 3), (1, 4), (0, 6), (0, 7),
    (2, 4), (1, 5), (4, 3), (3, 4), (1, 6), (1, 7), (2, 5), (2, 6),
    (2, 7), (4, 4), (3, 5), (3, 6), (3, 7), (4, 5), (4, 6), (4, 7),
)


def entry(values, i):
    found = values[-1]
    for n, value in enumerate(values[:-1]):
        found = jnp.where(i == n, value, found)
    return found


def offset_at(b, g):
    far = entry(FAR, b)
    return far + 1 if g == 0 else -far


def wrap(i, n):
    return jnp.where(i < 0, i + n, jnp.where(i >= n, i - n, i))


def nt(a, b):
    return lax.dot_general(a, b, (((1,), (1,)), ((), ())), preferred_element_type=F32)


def nn(a, b):
    return jnp.dot(a, b, preferred_element_type=F32)


def kernel(
    tok_hbm, routes_hbm, rw_hbm, wg_hbm, wu_hbm, wd_hbm, cot_hbm,
    mixed_ref, grad_ref,
    tok, cot, routes, weights, wg, wu, wd,
    xs, xr, p1s, p1r, p2s, p2r, h1, h2, rs, rr, weigh_hi, weigh_lo, plain,
    in_sem, send_sem, x_sem, p1_sem, p2_sem, h1_sem, h2_sem, r_sem,
):
    dp = lax.axis_index("dp")
    ctx = lax.axis_index("ctx")
    z, y, x = dp // 2, ctx // 4, ctx % 4

    def await_bytes(ref, sem):
        pltpu.make_async_copy(ref, ref, sem).wait()

    barrier = pltpu.get_barrier_semaphore()

    def greet_dp(k, carry):
        pl.semaphore_signal(barrier, inc=1, device_id=wrap(dp + k, NDP) * 16 + ctx, device_id_type=LOGICAL)
        return carry

    def greet_ctx(k, carry):
        pl.semaphore_signal(barrier, inc=1, device_id=dp * 16 + wrap(ctx + k, 16), device_id_type=LOGICAL)
        return carry

    loads = [
        pltpu.make_async_copy(routes_hbm, routes, in_sem.at[5]),
        pltpu.make_async_copy(rw_hbm, weights, in_sem.at[6]),
        pltpu.make_async_copy(tok_hbm, tok, in_sem.at[0]),
        pltpu.make_async_copy(cot_hbm, cot, in_sem.at[1]),
        pltpu.make_async_copy(wg_hbm, wg.at[pl.ds(PAD, COLS)], in_sem.at[2]),
        pltpu.make_async_copy(wu_hbm, wu.at[pl.ds(PAD, COLS)], in_sem.at[3]),
        pltpu.make_async_copy(wd_hbm, wd.at[pl.ds(PAD, COLS)], in_sem.at[4]),
    ]
    for load in loads:
        load.start()
    lax.fori_loop(1, NDP, greet_dp, 0)
    lax.fori_loop(1, 16, greet_ctx, 0)

    loads[0].wait()
    loads[1].wait()
    r0, r1 = routes[0:1].astype(F32), routes[1:2].astype(F32)
    w0, w1 = weights[0:1], weights[1:2]
    rows = routes.shape[1]
    experts = lax.broadcasted_iota(jnp.int32, (NDP, rows), 0).astype(F32)
    oh0 = (r0 == experts).astype(F32)
    oh1 = (r1 == experts).astype(F32)
    earlier = (
        lax.broadcasted_iota(jnp.int32, (rows, rows), 0)
        < lax.broadcasted_iota(jnp.int32, (rows, rows), 1)
    ).astype(F32)
    before = nn((oh0 + oh1).astype(BF), earlier.astype(BF))
    s0 = jnp.sum(before * oh0, axis=0, keepdims=True)
    s1 = jnp.sum(before * oh1, axis=0, keepdims=True)
    places = lax.broadcasted_iota(jnp.int32, (NDP * CAP, rows), 0).astype(F32)
    hit0 = (r0 * CAP + s0 == places).astype(F32)
    hit1 = (r1 * CAP + s1 == places).astype(F32)
    loads[2].wait()
    loads[3].wait()
    tok_f, cot_f = tok[...].astype(F32), cot[...].astype(F32)
    both = jnp.concatenate(
        [
            jnp.concatenate([tok_f, tok_f], axis=1),
            jnp.concatenate([cot_f * w0, cot_f * w1], axis=1),
        ],
        axis=0,
    ).astype(BF)
    pick = jnp.concatenate([hit0, hit1], axis=1).astype(BF)
    xs[...] = nt(pick, both).astype(BF).reshape(NDP, CAP, PAIR)

    pl.semaphore_wait(barrier, NDP - 1 + 15)

    def z_send(src, dst, dst_dp, kind, recv):
        pltpu.make_async_remote_copy(
            src_ref=src, dst_ref=dst, send_sem=send_sem.at[kind], recv_sem=recv,
            device_id=dst_dp * 16 + ctx, device_id_type=LOGICAL,
        ).start()

    def dispatch(b, carry):
        for g in range(2):
            off = offset_at(b, g)
            for c in range(2):
                dst = (wrap(z - off, NZ)) * 2 + c

                @pl.when(dst != dp)
                def _():
                    z_send(xs.at[dst], xr.at[dp], dst, 0, x_sem.at[2 * b + g])

        return carry

    lax.fori_loop(0, NB, dispatch, 0)
    xr[dp] = xs[dp]

    zero = jnp.zeros((PAD, FF), BF)
    for w in (wg, wu, wd):
        w[0:PAD] = zero
        w[PAD + COLS :] = zero
    weighted = (hit0 * w0 + hit1 * w1).T
    high = weighted.astype(BF)
    weigh_hi[...] = high
    weigh_lo[...] = (weighted - high.astype(F32)).astype(BF)
    plain[...] = (hit0 + hit1).T.astype(BF)
    for load in loads[4:]:
        load.wait()

    x_at = [wrap(x + d, 4) for d in range(4)]
    y_at = [wrap(y + d, 4) for d in range(4)]
    peers = {
        True: [dp * 16 + y * 4 + x_at[d] for d in range(1, 4)],
        False: [dp * 16 + y_at[d] * 4 + x for d in range(1, 4)],
    }

    def send(src, dst, kind, recv, along_x, d):
        pltpu.make_async_remote_copy(
            src_ref=src, dst_ref=dst, send_sem=send_sem.at[kind], recv_sem=recv,
            device_id=peers[along_x][d - 1], device_id_type=LOGICAL,
        ).start()

    def first(g, d=0):
        return x_at[d] if g == 0 else y_at[d]

    def second(g, d=0):
        return y_at[d] if g == 0 else x_at[d]

    def products(b):
        await_bytes(xr.at[pl.ds(0, 2)], x_sem.at[2 * b])

        here = offset_at(b, 1) == 0

        @pl.when(here)
        def _():
            await_bytes(xr.at[pl.ds(0, 1)], x_sem.at[2 * b + 1])

        @pl.when(jnp.logical_not(here))
        def _():
            await_bytes(xr.at[pl.ds(0, 2)], x_sem.at[2 * b + 1])

        block = jnp.concatenate(
            [
                xr[pl.ds(2 * (wrap(z + offset_at(b, g), NZ)), 2)].reshape(2 * CAP, PAIR)
                for g in range(2)
            ],
            axis=0,
        )
        left, right = block[:, 0:512], block[:, 384:896]
        parts = (
            nn(left, wg[PAD : PAD + 512]),
            nn(left, wu[PAD : PAD + 512]),
            nn(right, wd[0:512]),
        )
        for g in range(2):
            for p in range(4):
                for a in range(3):
                    p1s[b, g, p, :, a * 256 : a * 256 + 256] = parts[a][
                        g * 32 : g * 32 + 32, p * 256 : p * 256 + 256
                    ].astype(BF)
        for d in range(1, 4):
            for g in range(2):
                send(
                    p1s.at[b, g, first(g, d)], p1r.at[b, g, d - 1], 1, p1_sem.at[b], g == 0, d
                )

    def add_first(b):
        await_bytes(p1r.at[b], p1_sem.at[b])
        for g in range(2):
            total = p1s[b, g, first(g)].astype(F32)
            for d in range(3):
                total = total + p1r[b, g, d].astype(F32)
            for q in range(4):
                for a in range(3):
                    lane = a * 256 + 128 * (q % 2)
                    p2s[b, g, q, :, a * 128 : a * 128 + 128] = total[
                        16 * (q // 2) : 16 * (q // 2) + 16, lane : lane + 128
                    ].astype(BF)
        for d in range(1, 4):
            for g in range(2):
                send(
                    p2s.at[b, g, second(g, d)], p2r.at[b, g, d - 1], 2, p2_sem.at[b], g == 1, d
                )

    def add_second(b):
        await_bytes(p2r.at[b], p2_sem.at[b])
        for g in range(2):
            total = p2s[b, g, second(g)].astype(F32)
            for d in range(3):
                total = total + p2r[b, g, d].astype(F32)
            gate, up, hidden_grad = total[:, 0:128], total[:, 128:256], total[:, 256:384]
            sig = jax.nn.sigmoid(gate)
            h1[b, g, second(g), :, 0:128] = (gate * sig * up).astype(BF)
            h1[b, g, second(g), :, 128:256] = (
                hidden_grad * up * sig * (1.0 + gate * (1.0 - sig))
            ).astype(BF)
            h1[b, g, second(g), :, 256:384] = (hidden_grad * gate * sig).astype(BF)
        for d in range(1, 4):
            for g in range(2):
                mine = h1.at[b, g, second(g)]
                send(mine, mine, 3, h1_sem.at[b], g == 1, d)

    def spread(b):
        await_bytes(p2r.at[b], h1_sem.at[b])
        for d in range(1, 4):
            for g in range(2):
                send(h1.at[b, g], h2.at[b, g, first(g)], 4, h2_sem.at[b], g == 0, d)
        for g in range(2):
            h2[b, g, first(g)] = h1[b, g]

    def give_back(b):
        await_bytes(p1r.at[b], h2_sem.at[b])

        def whole(a):
            return jnp.concatenate(
                [
                    jnp.concatenate(
                        [
                            h2[b, g, p, 2 * half + q, :, a * 128 : a * 128 + 128]
                            for p in range(4)
                            for q in range(2)
                        ],
                        axis=1,
                    )
                    for g in range(2)
                    for half in range(2)
                ],
                axis=0,
            )

        out = nt(whole(0), wd[PAD : PAD + 512])
        row_grad = nt(whole(1), wg[0:512]) + nt(whole(2), wu[0:512])
        pair = jnp.concatenate(
            [out[:, 0:384], out[:, 384:512] + row_grad[:, 0:128], row_grad[:, 128:512]], axis=1
        ).astype(BF)
        for g in range(2):
            off = offset_at(b, g)
            for c in range(2):
                dst = (wrap(z + off, NZ)) * 2 + c
                at = (2 * g + c) * CAP
                rs[dst] = pair[at : at + CAP]

                @pl.when(dst != dp)
                def _():
                    z_send(rs.at[dst], rr.at[dp], dst, 5, r_sem.at[0])

    stages = (products, add_first, add_second, spread, give_back)

    def step(n, carry):
        code = entry(tuple(s * NB + b for s, b in PLAN), n)
        for s, work in enumerate(stages):

            @pl.when((code >= s * NB) & (code < s * NB + NB))
            def _():
                work(code - s * NB)

        return carry

    lax.fori_loop(0, len(PLAN), step, 0)
    rr[dp] = rs[dp]

    await_bytes(rr.at[pl.ds(0, NDP - 1)], r_sem.at[0])
    back = rr[...].reshape(NDP * CAP, PAIR)
    mixed = nn(weigh_hi[...], back[:, 0:512]) + nn(weigh_lo[...], back[:, 0:512])
    grad = nn(plain[...], back[:, 384:896])
    mixed_ref[...] = mixed.T[0:COLS].astype(BF)
    grad_ref[...] = grad.T[PAD:].astype(BF)

    await_bytes(xs.at[pl.ds(0, NDP - 1)], send_sem.at[0])
    await_bytes(p1r, send_sem.at[1])
    await_bytes(p2r, send_sem.at[2])
    await_bytes(p2r, send_sem.at[3])
    await_bytes(p1r, send_sem.at[4])
    await_bytes(xs.at[pl.ds(0, NDP - 1)], send_sem.at[5])


def shards(tokens, routes, route_weights, w_gate, w_up, w_down, cotangent):
    rows, cols = tokens.shape
    hbm = pl.BlockSpec(memory_space=pltpu.HBM)
    vmem = pl.BlockSpec(memory_space=pltpu.VMEM)
    dma = pltpu.SemaphoreType.DMA
    out = jax.ShapeDtypeStruct((cols, rows), BF)
    mixed, grad = pl.pallas_call(
        kernel,
        out_shape=(out, out),
        in_specs=[hbm, hbm, hbm, hbm, hbm, hbm, hbm],
        out_specs=(vmem, vmem),
        scratch_shapes=[
            pltpu.VMEM((cols, rows), BF),
            pltpu.VMEM((cols, rows), BF),
            pltpu.VMEM(routes.shape[::-1], jnp.int32),
            pltpu.VMEM(routes.shape[::-1], F32),
            pltpu.VMEM((PAD + COLS + PAD, FF), BF),
            pltpu.VMEM((PAD + COLS + PAD, FF), BF),
            pltpu.VMEM((PAD + COLS + PAD, FF), BF),
            pltpu.VMEM((NDP, CAP, PAIR), BF),
            pltpu.VMEM((NDP, CAP, PAIR), BF),
            pltpu.VMEM((NB, 2, 4, 32, 768), BF),
            pltpu.VMEM((NB, 2, 3, 32, 768), BF),
            pltpu.VMEM((NB, 2, 4, 16, 384), BF),
            pltpu.VMEM((NB, 2, 3, 16, 384), BF),
            pltpu.VMEM((NB, 2, 4, 16, 384), BF),
            pltpu.VMEM((NB, 2, 4, 4, 16, 384), BF),
            pltpu.VMEM((NDP, CAP, PAIR), BF),
            pltpu.VMEM((NDP, CAP, PAIR), BF),
            pltpu.VMEM((rows, NDP * CAP), BF),
            pltpu.VMEM((rows, NDP * CAP), BF),
            pltpu.VMEM((rows, NDP * CAP), BF),
            dma((7,)),
            dma((6,)),
            dma((NZ,)),
            dma((NB,)),
            dma((NB,)),
            dma((NB,)),
            dma((NB,)),
            dma((1,)),
        ],
        compiler_params=pltpu.CompilerParams(
            collective_id=0, has_side_effects=True, vmem_limit_bytes=63 << 20
        ),
        cost_estimate=pl.CostEstimate(
            flops=6 * 2 * 512 * COLS * FF, bytes_accessed=4 << 20, transcendentals=1 << 16
        ),
    )(tokens.T, routes.T, route_weights.T, w_gate[0], w_up[0], w_down[0].T, cotangent.T)
    return mixed.T, grad.T


def solution(mesh):
    in_specs = (
        P("dp", "ctx"),
        P("dp", None),
        P("dp", None),
        P("dp", "ctx", None),
        P("dp", "ctx", None),
        P("dp", None, "ctx"),
        P("dp", "ctx"),
    )
    out_specs = (P("dp", "ctx"), P("dp", "ctx"))
    return jax.shard_map(shards, mesh=mesh, in_specs=in_specs, out_specs=out_specs, check_vma=False)
```

time: 112 us -> 106 us (0.946)
  the two profiles are of different devices: /device:TPU:97 before, /device:TPU:1 now
where the time goes in v2:
time: 106 us
  Pallas kernels  103 us (97%)
  local copies, waits for them, and re-layouts  2.24 us (2%)
    pallas_call x1, Pallas kernels, shards(): pl.pallas_call(kernel, out_shape=(out, out), in_specs=[hbm, hbm, hbm, hbm...  103 us
    unnamed x4, local copies, waits for them, and re-layouts  2.24 us

profile of v2, /device:TPU:1, one launch (start us, length us, event | category | flops | bytes accessed | tf_op | source)
XLA Modules:
  0.0 106.3 jit_solution(3134729073988326021)
XLA Ops:
  0.6 103.4 %shard_map.86 = (bf16[448,128]{1,0:T(8,128)(2,1)}, bf16[448,128]{1,0:T(8,128)(2,1)}) custom-call(bf16[448,128]{1,0:T(8,128)(2,1)} %bitcast.16, s32[2,128]{1,0:T(2,128)} %bitcast.18, f32[2,128]{1,0:T(2,128)} %bitcast.19, bf16[448,1024]{1,0:T(8,128)(2,1)} %bitcast.13, bf16[448,1024]{1,0:T(8,128)(2,1)} %bitcast.14, bf16[448,1024]{1,0:T(8,128)(2,1)} %bitcast.15, ...), custom_call_target="tpu_custom_call" | custom-call | flops 2818572288 | bytes 4194304 | tf_op jit(solution)/shard_map/pallas_call | solution.py:335
  104.0 0.0 copy-start
  104.0 1.6 %copy.11 = bf16[128,448]{0,1:T(8,128)(2,1)} copy(bf16[128,448]{0,1:T(8,128)(2,1)} %bitcast.12) | data formatting | bytes 229376
  105.6 0.0 copy-done
  105.6 0.6 copy.12
Async XLA Ops:
  104.0 1.6 %copy-start = (bf16[448,128]{1,0:T(8,128)(2,1)S(1)}, bf16[448,128]{1,0:T(8,128)(2,1)}, u32[]{:S(2)}) copy-start(bf16[448,128]{1,0:T(8,128)(2,1)} %get-tuple-element.5) | copy-start | bytes 344068

commit v3 on v2

--- a/solution.py
+++ b/solution.py
@@ -15,6 +15,7 @@
 NDP = 32
 CAP = 16
 NB = 8
+EARLY = 7
 COLS = 448
 PAIR = 2 * COLS
 FF = 1024
@@ -57,14 +58,14 @@
 
 def kernel(
     tok_hbm, routes_hbm, rw_hbm, wg_hbm, wu_hbm, wd_hbm, cot_hbm,
-    mixed_ref, grad_ref,
+    out_ref,
     tok, cot, routes, weights, wg, wu, wd,
     xs, xr, p1s, p1r, p2s, p2r, h1, h2, rs, rr, weigh_hi, weigh_lo, plain,
     in_sem, send_sem, x_sem, p1_sem, p2_sem, h1_sem, h2_sem, r_sem,
 ):
     dp = lax.axis_index("dp")
     ctx = lax.axis_index("ctx")
-    z, y, x = dp // 2, ctx // 4, ctx % 4
+    z, core, y, x = dp // 2, dp % 2, ctx // 4, ctx % 4
 
     def await_bytes(ref, sem):
         pltpu.make_async_copy(ref, ref, sem).wait()
@@ -108,9 +109,10 @@
     before = nn((oh0 + oh1).astype(BF), earlier.astype(BF))
     s0 = jnp.sum(before * oh0, axis=0, keepdims=True)
     s1 = jnp.sum(before * oh1, axis=0, keepdims=True)
+    c0, c1 = r0 * CAP + s0, r1 * CAP + s1
     places = lax.broadcasted_iota(jnp.int32, (NDP * CAP, rows), 0).astype(F32)
-    hit0 = (r0 * CAP + s0 == places).astype(F32)
-    hit1 = (r1 * CAP + s1 == places).astype(F32)
+    hit0 = (c0 == places).astype(F32)
+    hit1 = (c1 == places).astype(F32)
     loads[2].wait()
     loads[3].wait()
     tok_f, cot_f = tok[...].astype(F32), cot[...].astype(F32)
@@ -136,7 +138,7 @@
         for g in range(2):
             off = offset_at(b, g)
             for c in range(2):
-                dst = (wrap(z - off, NZ)) * 2 + c
+                dst = wrap(z - off, NZ) * 2 + c
 
                 @pl.when(dst != dp)
                 def _():
@@ -151,6 +153,17 @@
     for w in (wg, wu, wd):
         w[0:PAD] = zero
         w[PAD + COLS :] = zero
+    pair_places = lax.broadcasted_iota(jnp.int32, (2 * CAP, rows), 0)
+    places = jnp.concatenate(
+        [
+            (pair_places + wrap(z - off, NZ) * 2 * CAP).astype(F32)
+            for far in FAR
+            for off in (far + 1, -far)
+        ],
+        axis=0,
+    )
+    hit0 = (c0 == places).astype(F32)
+    hit1 = (c1 == places).astype(F32)
     weighted = (hit0 * w0 + hit1 * w1).T
     high = weighted.astype(BF)
     weigh_hi[...] = high
@@ -193,7 +206,7 @@
 
         block = jnp.concatenate(
             [
-                xr[pl.ds(2 * (wrap(z + offset_at(b, g), NZ)), 2)].reshape(2 * CAP, PAIR)
+                xr[pl.ds(2 * wrap(z + offset_at(b, g), NZ), 2)].reshape(2 * CAP, PAIR)
                 for g in range(2)
             ],
             axis=0,
@@ -285,16 +298,18 @@
         pair = jnp.concatenate(
             [out[:, 0:384], out[:, 384:512] + row_grad[:, 0:128], row_grad[:, 128:512]], axis=1
         ).astype(BF)
+        late = jnp.where(b < EARLY, 0, 1)
         for g in range(2):
             off = offset_at(b, g)
+            back = 2 * (2 * b + g) + core
             for c in range(2):
-                dst = (wrap(z + off, NZ)) * 2 + c
+                dst = wrap(z + off, NZ) * 2 + c
                 at = (2 * g + c) * CAP
                 rs[dst] = pair[at : at + CAP]
 
                 @pl.when(dst != dp)
                 def _():
-                    z_send(rs.at[dst], rr.at[dp], dst, 5, r_sem.at[0])
+                    z_send(rs.at[dst], rr.at[back], dst, 5, r_sem.at[late])
 
     stages = (products, add_first, add_second, spread, give_back)
 
@@ -309,14 +324,20 @@
         return carry
 
     lax.fori_loop(0, len(PLAN), step, 0)
-    rr[dp] = rs[dp]
-
-    await_bytes(rr.at[pl.ds(0, NDP - 1)], r_sem.at[0])
-    back = rr[...].reshape(NDP * CAP, PAIR)
-    mixed = nn(weigh_hi[...], back[:, 0:512]) + nn(weigh_lo[...], back[:, 0:512])
-    grad = nn(plain[...], back[:, 384:896])
-    mixed_ref[...] = mixed.T[0:COLS].astype(BF)
-    grad_ref[...] = grad.T[PAD:].astype(BF)
+    rr[2 * (2 * FAR.index(0) + 1) + core] = rs[dp]
+
+    def summed(first, last):
+        back = rr[4 * first : 4 * last].reshape((last - first) * 4 * CAP, PAIR)
+        part = pl.ds(first * 4 * CAP, (last - first) * 4 * CAP)
+        mixed = nn(weigh_hi[:, part], back[:, 0:512]) + nn(weigh_lo[:, part], back[:, 0:512])
+        return mixed, nn(plain[:, part], back[:, 384:896])
+
+    await_bytes(rr.at[pl.ds(0, 4 * EARLY)], r_sem.at[0])
+    mixed, grad = summed(0, EARLY)
+    await_bytes(rr.at[pl.ds(0, 4 * (NB - EARLY) - 1)], r_sem.at[1])
+    mixed_late, grad_late = summed(EARLY, NB)
+    out_ref[0] = (mixed + mixed_late).T[0:COLS].astype(BF)
+    out_ref[1] = (grad + grad_late).T[PAD:].astype(BF)
 
     await_bytes(xs.at[pl.ds(0, NDP - 1)], send_sem.at[0])
     await_bytes(p1r, send_sem.at[1])
@@ -331,12 +352,12 @@
     hbm = pl.BlockSpec(memory_space=pltpu.HBM)
     vmem = pl.BlockSpec(memory_space=pltpu.VMEM)
     dma = pltpu.SemaphoreType.DMA
-    out = jax.ShapeDtypeStruct((cols, rows), BF)
-    mixed, grad = pl.pallas_call(
+    out = jax.ShapeDtypeStruct((2, cols, rows), BF)
+    both = pl.pallas_call(
         kernel,
-        out_shape=(out, out),
+        out_shape=out,
         in_specs=[hbm, hbm, hbm, hbm, hbm, hbm, hbm],
-        out_specs=(vmem, vmem),
+        out_specs=vmem,
         scratch_shapes=[
             pltpu.VMEM((cols, rows), BF),
             pltpu.VMEM((cols, rows), BF),
@@ -365,7 +386,7 @@
             dma((NB,)),
             dma((NB,)),
             dma((NB,)),
-            dma((1,)),
+            dma((2,)),
         ],
         compiler_params=pltpu.CompilerParams(
             collective_id=0, has_side_effects=True, vmem_limit_bytes=63 << 20
@@ -374,7 +395,7 @@
             flops=6 * 2 * 512 * COLS * FF, bytes_accessed=4 << 20, transcendentals=1 << 16
         ),
     )(tokens.T, routes.T, route_weights.T, w_gate[0], w_up[0], w_down[0].T, cotangent.T)
-    return mixed.T, grad.T
+    return both[0].T, both[1].T
 
 
 def solution(mesh):

time: 106 us -> 106 us (level)
    unnamed x4 -> x0, local copies, waits for them, and re-layouts: 2.24 us -> none
    transpose x0 -> x1, local copies, waits for them, and re-layouts: none -> 1.65 us  [shards(): return (both[0].T, both[1].T)]
where the time goes in v3:
time: 106 us
  Pallas kernels  103 us (97%)
  local copies, waits for them, and re-layouts  1.65 us (2%)
    pallas_call x1, Pallas kernels, shards(): pl.pallas_call(kernel, out_shape=out, in_specs=[hbm, hbm, hbm, hbm, hbm,...  103 us

profile of v3, /device:TPU:1, one launch (start us, length us, event | category | flops | bytes accessed | tf_op | source)
XLA Modules:
  0.0 105.7 jit_solution(233507990094381930)
XLA Ops:
  0.6 103.4 %shard_map.86 = bf16[2,448,128]{2,1,0:T(8,128)(2,1)} custom-call(bf16[448,128]{1,0:T(8,128)(2,1)} %bitcast.20, s32[2,128]{1,0:T(2,128)} %bitcast.22, f32[2,128]{1,0:T(2,128)} %bitcast.23, bf16[448,1024]{1,0:T(8,128)(2,1)} %bitcast.17, bf16[448,1024]{1,0:T(8,128)(2,1)} %bitcast.18, bf16[448,1024]{1,0:T(8,128)(2,1)} %bitcast.19, bf16[448,128]{1,0:T(8,128)(2,1)} %bitcast.21), custom_call_target="tpu_custom_call" | custom-call | flops 2818572288 | bytes 4194304 | tf_op jit(solution)/shard_map/pallas_call | solution.py:356
  104.1 1.7 %slice_bitcast_fusion = (bf16[128,448]{0,1:T(8,128)(2,1)}, bf16[128,448]{0,1:T(8,128)(2,1)}) fusion(bf16[2,448,128]{2,1,0:T(8,128)(2,1)} %shard_map.86), kind=kLoop, calls=%fused_computation | loop fusion | bytes 458752 | tf_op jit(solution)/shard_map/transpose | solution.py:398

commit v4 on v3

--- a/solution.py
+++ b/solution.py
@@ -33,6 +33,8 @@
 
 
 def entry(values, i):
+    if isinstance(i, int):
+        return values[i]
     found = values[-1]
     for n, value in enumerate(values[:-1]):
         found = jnp.where(i == n, value, found)
@@ -194,7 +196,7 @@
     def products(b):
         await_bytes(xr.at[pl.ds(0, 2)], x_sem.at[2 * b])
 
-        here = offset_at(b, 1) == 0
+        here = jnp.asarray(offset_at(b, 1) == 0)
 
         @pl.when(here)
         def _():
@@ -313,17 +315,8 @@
 
     stages = (products, add_first, add_second, spread, give_back)
 
-    def step(n, carry):
-        code = entry(tuple(s * NB + b for s, b in PLAN), n)
-        for s, work in enumerate(stages):
-
-            @pl.when((code >= s * NB) & (code < s * NB + NB))
-            def _():
-                work(code - s * NB)
-
-        return carry
-
-    lax.fori_loop(0, len(PLAN), step, 0)
+    for s, b in PLAN:
+        stages[s](b)
     rr[2 * (2 * FAR.index(0) + 1) + core] = rs[dp]
 
     def summed(first, last):

time: 106 us -> 105 us (level)
  no operation moved by 1% of the time
where the time goes in v4:
time: 105 us
  Pallas kernels  103 us (98%)
  local copies, waits for them, and re-layouts  1.65 us (2%)
    pallas_call x1, Pallas kernels, shards(): pl.pallas_call(kernel, out_shape=out, in_specs=[hbm, hbm, hbm, hbm, hbm,...  103 us

profile of v4, /device:TPU:1, one launch (start us, length us, event | category | flops | bytes accessed | tf_op | source)
XLA Modules:
  0.0 105.1 jit_solution(6095908046918528296)
XLA Ops:
  0.6 102.8 %shard_map.86 = bf16[2,448,128]{2,1,0:T(8,128)(2,1)} custom-call(bf16[448,128]{1,0:T(8,128)(2,1)} %bitcast.20, s32[2,128]{1,0:T(2,128)} %bitcast.22, f32[2,128]{1,0:T(2,128)} %bitcast.23, bf16[448,1024]{1,0:T(8,128)(2,1)} %bitcast.17, bf16[448,1024]{1,0:T(8,128)(2,1)} %bitcast.18, bf16[448,1024]{1,0:T(8,128)(2,1)} %bitcast.19, bf16[448,128]{1,0:T(8,128)(2,1)} %bitcast.21), custom_call_target="tpu_custom_call" | custom-call | flops 2818572288 | bytes 4194304 | tf_op jit(solution)/shard_map/pallas_call | solution.py:349
  103.4 1.7 %slice_bitcast_fusion = (bf16[128,448]{0,1:T(8,128)(2,1)}, bf16[128,448]{0,1:T(8,128)(2,1)}) fusion(bf16[2,448,128]{2,1,0:T(8,128)(2,1)} %shard_map.86), kind=kLoop, calls=%fused_computation | loop fusion | bytes 458752 | tf_op jit(solution)/shard_map/transpose | solution.py:391
